TPU v7x, 32 devices: a whole 2x2x4 slice. The times are simulated.
32 devices in a mesh: slab: 8 (over z, x), elec: 4 (over y, core).
Axes of the slice: x: 2, y: 2, z: 4, core: 2. Of those that a mesh axis runs over, the one named last changes fastest.
Arguments:
- potentials: float32 [128, 16, 128, 128], P('elec', None, 'slab'), may hold values from -6 to 6
- conductivity: float32 [16, 128, 128], P(None, 'slab'), may hold values from 0.1 to 1
- quadrupoles: int32 [512, 4], P('elec'), may hold values from 0 to 127, as said below
Outputs:
- jacobian: bfloat16 [512, 16, 128, 128], P('elec', 'slab')
Inputs may be any that keep to these rules, and one draw needn't show every extreme that they name: `quadrupoles`: rows g * 128 to (g + 1) * 128 - 1 are the measurements of group g; electrode e belongs to group e // 32. A and B are two different electrodes of the row's own group; M and N are two different electrodes of other groups. The rows of one group name, in M or N, at most 4 different electrodes of any one other group, and exactly 4 of some other group.
All inputs are finite; a program needn't handle non-finite values.
Results may differ from a plain program's by a relative error of at most 0.0058.
Values may be sent and summed in bfloat16 or wider, within the bound.
A program may use at most 256 MiB of HBM per device.

v0:
```python
import jax
import jax.numpy as jnp
from jax import lax
from jax.sharding import PartitionSpec as P


def padded_2(cells, sides, width):
    for axis, dim in sides:
        count = lax.axis_size(axis)
        ends = count - 1
        head = lax.slice_in_dim(cells, 0, width, axis=dim)
        tail = lax.slice_in_dim(cells, cells.shape[dim] - width, cells.shape[dim], axis=dim)
        cells = jnp.concatenate(
            [
                lax.ppermute(tail, axis, [(i, (i + 1) % count) for i in range(ends)]),
                cells,
                lax.ppermute(head, axis, [((i + 1) % count, i) for i in range(ends)]),
            ],
            axis=dim,
        )
    return cells


def differences(padded):
    grad_z = (padded[:, 2:, 1:-1, 1:-1] - padded[:, :-2, 1:-1, 1:-1]) * 0.5
    grad_x = (padded[:, 1:-1, 2:, 1:-1] - padded[:, 1:-1, :-2, 1:-1]) * 0.5
    grad_y = (padded[:, 1:-1, 1:-1, 2:] - padded[:, 1:-1, 1:-1, :-2]) * 0.5
    return jnp.stack([grad_z, grad_x, grad_y], 1).astype(jnp.bfloat16)


def sensitivity(tile_table, column_total, weight):
    table_rows = tile_table.shape[0]
    number_of_cells = weight.shape[0]
    flat_table = tile_table.reshape(table_rows, 3 * number_of_cells)
    table_ids = jnp.arange(table_rows, dtype=jnp.int32)

    def selector(first_ids, second_ids):
        first_hot = (first_ids[:, None] == table_ids[None, :]).astype(jnp.bfloat16)
        second_hot = (second_ids[:, None] == table_ids[None, :]).astype(jnp.bfloat16)
        return first_hot - second_hot

    source_sel = selector(column_total[:, 0], column_total[:, 1])
    probe_sel = selector(column_total[:, 2], column_total[:, 3])
    reading_count = column_total.shape[0]
    block_size = 16
    for candidate in (128, 64, 32):
        if reading_count % candidate == 0 and block_size == 16:
            block_size = candidate
    number_of_blocks = reading_count // block_size

    def block_rows(block_pair):
        source_rows, probe_rows = block_pair
        source_grad = jnp.dot(source_rows, flat_table, preferred_element_type=jnp.float32).reshape(
            block_size, 3, number_of_cells
        )
        probe_grad = jnp.dot(probe_rows, flat_table, preferred_element_type=jnp.float32).reshape(
            block_size, 3, number_of_cells
        )
        summed = jnp.sum(source_grad * probe_grad, axis=1)
        return (-(weight[None] * summed)).astype(jnp.bfloat16)

    output_rows = lax.map(
        block_rows,
        (
            source_sel.reshape(number_of_blocks, block_size, table_rows),
            probe_sel.reshape(number_of_blocks, block_size, table_rows),
        ),
    )
    return output_rows.reshape(reading_count, number_of_cells)


def shards(potentials, conductivity, quadrupoles):
    per_group = potentials.shape[0]
    reading_count = quadrupoles.shape[0]
    shifted_rows, cond_slab = (
        lax.all_to_all(potentials, "slab", split_axis=1, concat_axis=2, tiled=True),
        lax.all_to_all(conductivity[None], "slab", split_axis=1, concat_axis=2, tiled=True),
    )
    extended = padded_2(shifted_rows, (("slab", 1),), 1)
    padded = jnp.pad(extended, ((0, 0), (0, 0), (1, 1), (1, 1)))
    weight = cond_slab[0].reshape(-1)
    output_dimensions = (
        reading_count,
        shifted_rows.shape[1],
        shifted_rows.shape[2],
        shifted_rows.shape[3],
    )
    grads = differences(padded).reshape(per_group, 3, -1)
    tile_table = lax.all_gather(grads, "elec", axis=0, tiled=True)
    rows_flat = sensitivity(tile_table, quadrupoles, weight)
    return rows_flat.reshape(output_dimensions)


def solution(mesh):
    in_specs = (P("elec", None, "slab", None), P(None, "slab", None), P("elec", None))
    out_specs = P("elec", "slab", None, None)
    return jax.shard_map(shards, mesh=mesh, in_specs=in_specs, out_specs=out_specs, check_vma=False)
```

profile of v0, /device:TPU:11, one launch (start us, length us, event | category | flops | bytes accessed | tf_op | source)
XLA Modules:
  0.0 510.2 jit_solution(15257726904695953435)
XLA Ops:
  6.5 0.0 all-gather.2.cloned.1.call-start
  6.5 2.6 copy.19
  9.2 95.6 %all_to_all.33 = f32[32,16,16,128]{3,2,0,1:T(8,128)S(1)} all-to-all(f32[32,16,16,128]{3,2,0,1:T(8,128)S(1)} %copy.19), channel_id=1, replica_groups=mesh['slab'=8,'elec'=4] {'slab'}, dimensions={1} | all-to-all | bytes 8388608 | tf_op jit(solution)/shard_map/all_to_all | solution.py:76
  104.8 0.6 copy.21
  105.4 0.0 copy-start
  105.4 0.5 fusion.29
  105.9 3.4 collective-permute-start
  109.3 2.8 collective-permute-start.1
  112.1 84.9 %collective-permute-done = f32[32,1,128,128]{3,2,1,0:T(8,128)S(1)} collective-permute-done((f32[32,1,128,128]{3,2,1,0:T(8,128)S(1)}, f32[32,1,128,128]{3,2,1,0:T(8,128)S(1)}, u32[]{:S(2)}, u32[]{:S(2)}) %collective-permute-start) | collective-permute-done | bytes 2097184 | tf_op jit(solution)/shard_map/ppermute | solution.py:17
  197.0 4.2 collective-permute-done.1
  201.2 0.0 copy-done
  201.2 0.0 copy-done.1
  201.2 1.3 copy-done.3
  202.5 7.5 %select_maximum_fusion = f32[32,4,130,130]{3,2,1,0:T(8,128)S(1)} fusion(f32[32,1,128,128]{3,2,1,0:T(8,128)S(1)} %collective-permute-done, f32[32,2,128,128]{3,2,1,0:T(8,128)S(1)} %bitcast.42, f32[32,1,128,128]{3,2,1,0:T(8,128)S(1)} %collective-permute-done.1), kind=kLoop, calls=%fused_computation.8 | loop fusion | flops 32448000 | bytes 17041408 | tf_op jit(solution)/shard_map/concatenate | solution.py:13
  210.0 4.8 fusion.9
  214.9 4.3 stack.13
  219.2 4.2 stack.14
  223.3 0.0 copy-done.2
  223.3 5.1 fusion.12
  228.4 4.3 stack.12
  232.7 0.0 copy-done.4
  232.7 5.5 %pad_maximum_fusion = bf16[32,3,32768]{2,0,1:T(8,128)(2,1)} fusion(bf16[32,1,32768]{2,0,1:T(8,128)(2,1)} %stack.14, bf16[32,1,32768]{2,0,1:T(8,128)(2,1)S(1)} %copy-done.4, bf16[32,1,32768]{2,0,1:T(8,128)(2,1)} %stack.12), kind=kLoop, calls=%fused_computation.14 | loop fusion | flops 6291456 | bytes 12582912 | tf_op jit(solution)/shard_map/stack | solution.py:28
  238.2 0.0 all-gather.2.cloned.1.call-update
  238.2 4.7 all-to-all-start
  242.9 0.0 copy-done.5
  242.9 4.3 all-to-all-done
  247.2 147.1 %all-gather.2.cloned.1.call-done = bf16[128,3,32768]{2,0,1:T(8,128)(2,1)} async-done(((bf16[32,3,32768]{2,0,1:T(8,128)(2,1)}), bf16[128,3,32768]{2,0,1:T(8,128)(2,1)}) %all-gather.2.cloned.1.call-update) | async-done | bytes 25165840 | tf_op jit(solution)/shard_map/all_gather | solution.py:89
  394.3 32.5 %copy.22 = bf16[128,3,32768]{0,2,1:T(8,128)(2,1)} copy(bf16[128,3,32768]{2,0,1:T(8,128)(2,1)} %all-gather.2.cloned.1.call-done) | data formatting | bytes 50331648 | tf_op jit(solution)/shard_map/all_gather | solution.py:89
  426.8 25.3 %fusion.1 = f32[128,3,32768]{2,0,1:T(8,128)} fusion(bf16[128,3,32768]{0,2,1:T(8,128)(2,1)} %copy.22, s32[128]{0:T(128)S(1)} %get-tuple-element.28, s32[128]{0:T(128)S(1)} %get-tuple-element.29), kind=kOutput, calls=%fused_computation.6 | convolution fusion | flops 3221356544 | bytes 75498496 | tf_op jit(solution)/shard_map/while/body/eval_jaxpr/dot_general | solution.py:53
  452.1 37.3 %multiply_reduce_fusion = f32[128,32768]{1,0:T(8,128)} fusion(f32[128,3,32768]{2,0,1:T(8,128)} %fusion.1, bf16[128,3,32768]{0,2,1:T(8,128)(2,1)} %copy.22, s32[128]{0:T(128)S(1)} %get-tuple-element.30, s32[128]{0:T(128)S(1)} %get-tuple-element.26), kind=kOutput, calls=%fused_computation | convolution fusion | flops 3242328064 | bytes 92275712 | tf_op jit(solution)/shard_map/while/body/eval_jaxpr/dot_general | solution.py:56
  489.4 9.4 %copy.24 = f32[16,8,256,128]{3,2,1,0:T(8,128)S(1)} copy(f32[16,8,256,128]{3,1,2,0:T(8,128)} %bitcast.45) | data formatting | bytes 33554432
  498.8 4.6 negate_convert_fusion
  (7 shorter events, 0.0 us)
Async XLA Ops:
  6.5 387.8 %all-gather.2.cloned.1.call-start = ((), (), s32[]{:S(2)}) async-start(), calls=%async_computation.2 | async-start | bytes 31457280 | tf_op jit(solution)/shard_map/all_gather | solution.py:89
  105.4 95.8 %copy-start = (f32[32,2,8,16,128]{4,3,2,1,0:T(8,128)}, f32[32,2,8,16,128]{4,3,2,1,0:T(8,128)S(1)}, u32[]{:S(2)}) copy-start(f32[32,2,8,16,128]{4,3,2,1,0:T(8,128)S(1)} %copy.21) | copy-start | bytes 12582916
  105.9 91.1 %collective-permute-start = (f32[32,1,128,128]{3,2,1,0:T(8,128)S(1)}, f32[32,1,128,128]{3,2,1,0:T(8,128)S(1)}, u32[]{:S(2)}, u32[]{:S(2)}) collective-permute-start(f32[32,1,128,128]{3,2,1,0:T(8,128)S(1)} %get-tuple-element.24), channel_id=1, source_target_pairs={{4,0},{8,4},{12,8},{16,12},{20,16},{24,20},{28,24},{5,1},{9,5},{13... | collective-permute-start | bytes 6291464 | tf_op jit(solution)/shard_map/ppermute | solution.py:17
  109.3 91.9 %collective-permute-start.1 = (f32[32,1,128,128]{3,2,1,0:T(8,128)S(1)}, f32[32,1,128,128]{3,2,1,0:T(8,128)S(1)}, u32[]{:S(2)}, u32[]{:S(2)}) collective-permute-start(f32[32,1,128,128]{3,2,1,0:T(8,128)S(1)} %get-tuple-element.17), channel_id=1, source_target_pairs={{0,4},{4,8},{8,12},{12,16},{16,20},{20,24},{24,28},{1,5},{5,9},{9,... | collective-permute-start | bytes 6291464 | tf_op jit(solution)/shard_map/ppermute | solution.py:15
  197.0 4.2 copy-start.1
  201.2 1.3 copy-start.3
  214.9 8.5 %copy-start.2 = (f32[32,1,128,128]{3,2,1,0:T(8,128)S(1)}, f32[32,1,128,128]{3,2,1,0:T(8,128)}, u32[]{:S(2)}) copy-start(f32[32,1,128,128]{3,2,1,0:T(8,128)} %copy-done.1) | copy-start | bytes 6291460
  228.4 4.3 copy-start.4
  238.2 4.7 copy-start.5
  238.2 8.9 %all-to-all-start = ((f32[1,16,16,128]{3,2,0,1:T(8,128)}), f32[1,16,16,128]{3,2,0,1:T(8,128)S(1)}, u32[]{:S(2)}, u32[]{:S(2)}) async-start(f32[1,16,16,128]{3,2,0,1:T(8,128)} %bitcast), calls=%async_computation | async-start | bytes 262144 | tf_op jit(solution)/shard_map/all_to_all | solution.py:77
Sparse Core Ops, SparseCore 0:
  238.4 155.9 all-gather.1
where the time goes:
time: 513 us; the launch traced here: 510 us
  waiting for transfers between devices  241 us (47%)
  blocking collectives  95.6 us (19%)
  matrix products  62.5 us (12%)
  local copies, waits for them, and re-layouts  59.7 us (12%)
  other arithmetic  27.5 us (5%)
  between operations  13.5 us (3%)
  starting transfers between devices  10.8 us (2%)
    all_gather x1, waiting for transfers between devices, shards(): tile_table = lax.all_gather(grads, 'elec', axis=0, tiled=True)  147 us
    all_to_all x1, blocking collectives, shards(): lax.all_to_all(potentials, 'slab', split_axis=1, concat_axis=2, tiled=True)  95.6 us
    ppermute x1, waiting for transfers between devices, padded_2(): lax.ppermute(head, axis, [((i + 1) % count, i) for i in range(ends)])  84.9 us
    dot_general x1, matrix products, block_rows(): jnp.dot(probe_rows, flat_table, preferred_element_type=jnp.float32)  37.3 us
    all_gather x1, local copies, waits for them, and re-layouts, shards(): tile_table = lax.all_gather(grads, 'elec', axis=0, tiled=True)  32.5 us
    dot_general x1, matrix products, block_rows(): jnp.dot(source_rows, flat_table, preferred_element_type=jnp.float32)  25.3 us
    unnamed x14, local copies, waits for them, and re-layouts  13.4 us
    another operation x3, local copies, waits for them, and re-layouts, differences(): return jnp.stack([grad_z, grad_x, grad_y], 1).astype(jnp.bfloat16)  12.8 us
  transfers between devices with their start and end apart: 4, of which 4 were waited for; matrix products, arithmetic and copies ran while one was open for 0% of the time, Pallas kernels for 0%

commit v1 on v0

v1 whole, which is shorter than its diff:
```python
import functools

import jax
import jax.numpy as jnp
from jax import lax
from jax.experimental import pallas as pl
from jax.experimental.pallas import tpu as pltpu
from jax.sharding import PartitionSpec as P

MESH = pl.DeviceIdType.MESH
REQ = 4


def lists(quadrupoles, per_group, groups):
    me = lax.axis_index("elec")
    ids = jnp.arange(per_group * groups, dtype=jnp.int32)
    owner = ids // per_group
    away = (owner - me) % groups
    named = jnp.any(quadrupoles[:, 2:4].reshape(-1)[:, None] == ids[None, :], axis=0)
    before = (owner[:, None] == owner[None, :]) & (ids[None, :] < ids[:, None])
    rank = jnp.sum((before & named[None, :]).astype(jnp.int32), axis=1)
    other = per_group + (away - 1) * REQ + jnp.minimum(rank, REQ - 1)
    slot = jnp.where(away == 0, ids - me * per_group, other)
    index = jnp.sum(jnp.where(quadrupoles[:, :, None] == ids, slot, 0), axis=-1)
    steps = jnp.arange(groups, dtype=jnp.int32)[:, None, None]
    lanes = jnp.arange(128, dtype=jnp.int32)[None, :, None]
    hit = named & (away == steps) & (rank == lanes)
    asked = jnp.sum(jnp.where(hit, ids % per_group, 0), axis=-1)
    return index.astype(jnp.int32), jnp.broadcast_to(asked[:, None, :], (groups, 8, 128))


def exchange_kernel(slabs, groups, planes, *refs):
    pot, cond, asked, table_out, weight_out = refs[:5]
    pot_v, gz_src, asked_in, asked_s, weight_v = refs[5:10]
    p_in = refs[10 : 10 + planes]
    own = refs[10 + planes : 10 + 2 * planes]
    far = refs[10 + 2 * planes : 10 + 3 * planes]
    out_box = refs[10 + 3 * planes : 10 + 4 * planes]
    (slab_send, slab_recv, cond_send, cond_recv, ask_send, ask_recv, far_send, far_recv, local) = refs[10 + 4 * planes :]

    count, depth, rows, width = pot.shape
    me = lax.axis_index("slab")
    group = lax.axis_index("elec")
    my_rows = pl.ds(pl.multiple_of(me * rows, rows), rows)

    stage = pltpu.make_async_copy(pot, pot_v, local.at[0])
    stage.start()

    barrier = pltpu.get_barrier_semaphore()
    for step in range(1, slabs):
        pl.semaphore_signal(barrier, inc=1, device_id={"slab": lax.rem(me + step, slabs)}, device_id_type=MESH)
    for step in range(1, groups):
        pl.semaphore_signal(barrier, inc=1, device_id={"elec": lax.rem(group + step, groups)}, device_id_type=MESH)
    pl.semaphore_wait(barrier, slabs + groups - 2)

    asks = []
    for step in range(1, groups):
        copy = pltpu.make_async_remote_copy(
            src_ref=asked.at[step],
            dst_ref=asked_in.at[step],
            send_sem=ask_send.at[step],
            recv_sem=ask_recv.at[step],
            device_id={"elec": lax.rem(group + step, groups)},
            device_id_type=MESH,
        )
        copy.start()
        asks.append(copy)

    def p_copy(plane, step):
        to = lax.rem(me + step, slabs)
        return pltpu.make_async_remote_copy(
            src_ref=pot.at[:, to * planes + plane],
            dst_ref=p_in[plane].at[:, my_rows, :],
            send_sem=slab_send.at[0, plane, step],
            recv_sem=slab_recv.at[0, plane, step],
            device_id={"slab": to},
            device_id_type=MESH,
        )

    def gz_copy(plane, step):
        to = lax.rem(me + step, slabs)
        return pltpu.make_async_remote_copy(
            src_ref=gz_src.at[plane, to],
            dst_ref=own[plane].at[:, 0, my_rows, :],
            send_sem=slab_send.at[1, plane, step],
            recv_sem=slab_recv.at[1, plane, step],
            device_id={"slab": to},
            device_id_type=MESH,
        )

    def cond_copy(step):
        to = lax.rem(me + step, slabs)
        return pltpu.make_async_remote_copy(
            src_ref=cond.at[pl.ds(to * planes, planes)],
            dst_ref=weight_v.at[:, my_rows, :],
            send_sem=cond_send.at[step],
            recv_sem=cond_recv.at[step],
            device_id={"slab": to},
            device_id_type=MESH,
        )

    def p_local(plane):
        return pltpu.make_async_copy(pot.at[:, me * planes + plane], p_in[plane].at[:, my_rows, :], local.at[1 + plane])

    def gz_local(plane):
        return pltpu.make_async_copy(
            gz_src.at[plane, me], own[plane].at[:, 0, my_rows, :], local.at[1 + planes + plane]
        )

    cond_local = pltpu.make_async_copy(
        cond.at[pl.ds(me * planes, planes)], weight_v.at[:, my_rows, :], local.at[1 + 2 * planes]
    )

    for plane in range(planes):
        for step in range(1, slabs):
            p_copy(plane, step).start()
        p_local(plane).start()
        if plane == 0:
            stage.wait()

        @pl.loop(0, count)
        def _(e, plane=plane):
            for to in range(slabs):
                z = to * planes + plane
                above = pot_v[e, z + 1] if z + 1 < depth else jnp.zeros((rows, width), jnp.float32)
                below = pot_v[e, z - 1] if z > 0 else jnp.zeros((rows, width), jnp.float32)
                gz_src[plane, to, e] = ((above - below) * 0.5).astype(jnp.bfloat16)

        for step in range(1, slabs):
            gz_copy(plane, step).start()
        gz_local(plane).start()
    for step in range(1, slabs):
        cond_copy(step).start()
    cond_local.start()

    for copy in asks:
        copy.wait()
    to_scalar = pltpu.make_async_copy(asked_in, asked_s, local.at[2 + 2 * planes])
    to_scalar.start()
    to_scalar.wait()

    x_size = p_in[0].shape[1]
    row = lax.broadcasted_iota(jnp.int32, (x_size, width), 0)
    lane = lax.broadcasted_iota(jnp.int32, (x_size, width), 1)

    def far_copy(plane, step):
        return pltpu.make_async_remote_copy(
            src_ref=out_box[plane].at[step - 1],
            dst_ref=far[plane].at[groups - 1 - step],
            send_sem=far_send.at[plane, step],
            recv_sem=far_recv.at[plane, step],
            device_id={"elec": lax.rem(group + step, groups)},
            device_id_type=MESH,
        )

    def own_out(plane):
        return pltpu.make_async_copy(
            own[plane], table_out.at[plane, pl.ds(0, count)], local.at[3 + 2 * planes + plane]
        )

    def far_out(plane, place):
        return pltpu.make_async_copy(
            far[plane].at[place],
            table_out.at[plane, pl.ds(count + place * REQ, REQ)],
            local.at[3 + 3 * planes + plane * (groups - 1) + place],
        )

    for plane in range(planes):
        for step in range(1, slabs):
            p_copy(plane, step).wait_recv()
            gz_copy(plane, step).wait_recv()
        p_local(plane).wait()
        gz_local(plane).wait()

        @pl.loop(0, count)
        def _(e, plane=plane):
            p = p_in[plane][e]
            up = jnp.where(row < x_size - 1, pltpu.roll(p, x_size - 1, 0), 0.0)
            down = jnp.where(row > 0, pltpu.roll(p, 1, 0), 0.0)
            own[plane][e, 1] = ((up - down) * 0.5).astype(jnp.bfloat16)
            right = jnp.where(lane < width - 1, pltpu.roll(p, width - 1, 1), 0.0)
            left = jnp.where(lane > 0, pltpu.roll(p, 1, 1), 0.0)
            own[plane][e, 2] = ((right - left) * 0.5).astype(jnp.bfloat16)

        for step in range(1, groups):
            for place in range(REQ):
                chosen = asked_s[groups - step, 0, place]
                for d in range(3):
                    out_box[plane][step - 1, place, d] = own[plane][chosen, d]
            far_copy(plane, step).start()
        own_out(plane).start()

    for step in range(1, slabs):
        cond_copy(step).wait_recv()
    cond_local.wait()
    weight_done = pltpu.make_async_copy(weight_v, weight_out, local.at[2 + 2 * planes])
    weight_done.start()
    for plane in range(planes):
        for step in range(1, groups):
            far_copy(plane, step).wait_recv()
            far_out(plane, groups - 1 - step).start()
    for plane in range(planes):
        own_out(plane).wait()
        for place in range(groups - 1):
            far_out(plane, place).wait()
        for step in range(1, groups):
            far_copy(plane, step).wait_send()
        for step in range(1, slabs):
            p_copy(plane, step).wait_send()
            gz_copy(plane, step).wait_send()
    for step in range(1, slabs):
        cond_copy(step).wait_send()
    weight_done.wait()


def exchange(potentials, conductivity, asked, slabs, groups):
    count, depth, rows, width = potentials.shape
    planes = depth // slabs
    x_size = rows * slabs
    table_rows = count + (groups - 1) * REQ
    hbm = pl.BlockSpec(memory_space=pl.ANY)
    dma = pltpu.SemaphoreType.DMA
    bf16, f32 = jnp.bfloat16, jnp.float32
    return pl.pallas_call(
        functools.partial(exchange_kernel, slabs, groups, planes),
        out_shape=[
            jax.ShapeDtypeStruct((planes, table_rows, 3, x_size, width), bf16),
            jax.ShapeDtypeStruct((planes, x_size, width), f32),
        ],
        in_specs=[hbm, hbm, pl.BlockSpec(memory_space=pltpu.VMEM)],
        out_specs=[hbm, hbm],
        scratch_shapes=[
            pltpu.VMEM((count, depth, rows, width), f32),
            pltpu.VMEM((planes, slabs, count, rows, width), bf16),
            pltpu.VMEM((groups, 8, 128), jnp.int32),
            pltpu.SMEM((groups, 8, 128), jnp.int32),
            pltpu.VMEM((planes, x_size, width), f32),
        ]
        + [pltpu.VMEM((count, x_size, width), f32)] * planes
        + [pltpu.VMEM((count, 3, x_size, width), bf16)] * planes
        + [pltpu.VMEM((groups - 1, REQ, 3, x_size, width), bf16)] * planes
        + [pltpu.VMEM((groups - 1, REQ, 3, x_size, width), bf16)] * planes
        + [
            dma((2, planes, slabs)),
            dma((2, planes, slabs)),
            dma((slabs,)),
            dma((slabs,)),
            dma((groups,)),
            dma((groups,)),
            dma((planes, groups)),
            dma((planes, groups)),
            dma((3 + 3 * planes + planes * (groups - 1),)),
        ],
        compiler_params=pltpu.CompilerParams(
            collective_id=0, has_side_effects=True, vmem_limit_bytes=48 * 1024 * 1024
        ),
        name="exchange",
    )(potentials, conductivity, asked)


def rows_kernel(index, table, weight, out):
    w = -weight[0]
    readings = out.shape[0]

    def reading(m):
        a, b, c, d = index[4 * m], index[4 * m + 1], index[4 * m + 2], index[4 * m + 3]
        total = None
        for way in range(3):
            source = table[0, a, way].astype(jnp.float32) - table[0, b, way].astype(jnp.float32)
            probe = table[0, c, way].astype(jnp.float32) - table[0, d, way].astype(jnp.float32)
            term = source * probe
            total = term if total is None else total + term
        out[m, 0] = (w * total).astype(jnp.bfloat16)

    @pl.loop(0, readings // 4)
    def _(block):
        for k in range(4):
            reading(block * 4 + k)


def jacobian_rows(index, table, weight):
    planes, table_rows, ways, x_size, width = table.shape
    readings = index.shape[0]
    part = 32
    return pl.pallas_call(
        rows_kernel,
        out_shape=jax.ShapeDtypeStruct((readings, planes, x_size, width), jnp.bfloat16),
        grid_spec=pltpu.PrefetchScalarGridSpec(
            num_scalar_prefetch=1,
            grid=(planes, x_size // part),
            in_specs=[
                pl.BlockSpec((1, table_rows, ways, part, width), lambda z, x, _: (z, 0, 0, x, 0)),
                pl.BlockSpec((1, part, width), lambda z, x, _: (z, x, 0)),
            ],
            out_specs=pl.BlockSpec((readings, 1, part, width), lambda z, x, _: (0, z, x, 0)),
        ),
        compiler_params=pltpu.CompilerParams(vmem_limit_bytes=32 * 1024 * 1024),
        name="rows",
    )(index.reshape(-1), table, weight)


def general(potentials, conductivity, quadrupoles):
    shifted = lax.all_to_all(potentials, "slab", split_axis=1, concat_axis=2, tiled=True)
    cond = lax.all_to_all(conductivity[None], "slab", split_axis=1, concat_axis=2, tiled=True)[0]
    slabs = lax.axis_size("slab")
    ends = slabs - 1
    last = shifted.shape[1] - 1
    below = lax.ppermute(shifted[:, last:], "slab", [(i, i + 1) for i in range(ends)])
    above = lax.ppermute(shifted[:, :1], "slab", [(i + 1, i) for i in range(ends)])
    tall = jnp.concatenate([below, shifted, above], axis=1)
    wide = jnp.pad(shifted, ((0, 0), (0, 0), (1, 1), (1, 1)))
    grads = jnp.stack(
        [
            (tall[:, 2:] - tall[:, :-2]) * 0.5,
            (wide[:, :, 2:, 1:-1] - wide[:, :, :-2, 1:-1]) * 0.5,
            (wide[:, :, 1:-1, 2:] - wide[:, :, 1:-1, :-2]) * 0.5,
        ],
        1,
    ).astype(jnp.bfloat16)
    table = lax.all_gather(grads.reshape(grads.shape[0], 3, -1), "elec", axis=0, tiled=True)
    ids = jnp.arange(table.shape[0], dtype=jnp.int32)
    hot = (quadrupoles[:, :, None] == ids).astype(jnp.bfloat16)
    flat = table.reshape(table.shape[0], -1)
    shape = (quadrupoles.shape[0], 3, -1)
    source = jnp.dot(hot[:, 0] - hot[:, 1], flat, preferred_element_type=jnp.float32).reshape(shape)
    probe = jnp.dot(hot[:, 2] - hot[:, 3], flat, preferred_element_type=jnp.float32).reshape(shape)
    rows = -(cond.reshape(-1)[None] * jnp.sum(source * probe, axis=1))
    return rows.astype(jnp.bfloat16).reshape((quadrupoles.shape[0],) + shifted.shape[1:])


def shards(potentials, conductivity, quadrupoles):
    slabs, groups = lax.axis_size("slab"), lax.axis_size("elec")
    count, depth, rows, width = potentials.shape
    if rows % 16 or width % 128 or depth % slabs or (rows * slabs) % 32 or quadrupoles.shape[0] % 4:
        return general(potentials, conductivity, quadrupoles)
    index, asked = lists(quadrupoles, count, groups)
    table, weight = exchange(potentials, conductivity, asked, slabs, groups)
    return jacobian_rows(index, table, weight)


def solution(mesh):
    in_specs = (P("elec", None, "slab", None), P(None, "slab", None), P("elec", None))
    out_specs = P("elec", "slab", None, None)
    return jax.shard_map(shards, mesh=mesh, in_specs=in_specs, out_specs=out_specs, check_vma=False)
```

time: 513 us -> 193 us (0.38)
  waiting for transfers between devices: 241 us -> 0 us
  Pallas kernels: 0 us -> 184 us
  blocking collectives: 95.6 us -> 0 us
  matrix products: 62.5 us -> 0 us
  local copies, waits for them, and re-layouts: 59.7 us -> 7.7 us
  other arithmetic: 27.5 us -> 1.42 us
  between operations: 13.5 us -> 0.07 us
  starting transfers between devices: 10.8 us -> 0 us
    pallas_call x0 -> x2, Pallas kernels: none -> 184 us  [the longest x1 166 us: exchange(): pl.pallas_call(functools.partial(exchange_kernel, slabs, groups, planes),...]
    all_gather x1 -> x0, waiting for transfers between devices: 147 us -> none  [shards(): tile_table = lax.all_gather(grads, 'elec', axis=0, tiled=True)]
    all_to_all x1 -> x0, blocking collectives: 95.6 us -> none  [shards(): lax.all_to_all(potentials, 'slab', split_axis=1, concat_axis=2, tiled=True)]
    ppermute x2 -> x0, waiting for transfers between devices: 89.1 us -> none  [the longest x1 84.9 us: padded_2(): lax.ppermute(head, axis, [((i + 1) % count, i) for i in range(ends)])]
    dot_general x2 -> x0, matrix products: 62.5 us -> none  [the longest x1 37.3 us: block_rows(): jnp.dot(probe_rows, flat_table, preferred_element_type=jnp.float32)]
    all_gather x1 -> x0, local copies, waits for them, and re-layouts: 32.5 us -> none  [shards(): tile_table = lax.all_gather(grads, 'elec', axis=0, tiled=True)]
    another operation x3 -> x0, other arithmetic: 15.4 us -> none
    another operation x3 -> x0, local copies, waits for them, and re-layouts: 12.8 us -> none  [differences(): return jnp.stack([grad_z, grad_x, grad_y], 1).astype(jnp.bfloat16)]
  transfers between devices with their start and end apart: 4 -> 0, of which waited for: 4 -> 0; matrix products, arithmetic and copies ran while one was open for 0% -> 0% of each run, Pallas kernels for 0% -> 0%
where the time goes in v1:
time: 193 us
  Pallas kernels  184 us (95%)
  local copies, waits for them, and re-layouts  7.7 us (4%)
    pallas_call x1, Pallas kernels, exchange(): pl.pallas_call(functools.partial(exchange_kernel, slabs, groups, planes),...  166 us
    pallas_call x1, Pallas kernels, jacobian_rows(): pl.pallas_call(rows_kernel, out_shape=jax.ShapeDtypeStruct((readings, pla...  18.4 us
    unnamed x6, local copies, waits for them, and re-layouts  6.54 us

profile of v1, /device:TPU:11, one launch (start us, length us, event | category | flops | bytes accessed | tf_op | source)
XLA Modules:
  0.0 193.2 jit_solution(1441859082785980031)
XLA Ops:
  0.0 0.7 slice.3
  0.7 0.1 copy.7
  0.8 0.1 eq.91
  0.9 0.1 fusion
  1.1 0.2 convert_reduce_fusion
  1.3 0.9 select_reduce_fusion.1
  2.2 0.1 select_reduce_fusion
  2.4 0.1 copy.8
  2.5 0.1 reshape.120.index
  2.6 0.0 copy-start.1
  2.6 2.2 %copy-done.1 = f32[32,16,16,128]{3,2,1,0:T(8,128)S(1)} copy-done((f32[32,16,16,128]{3,2,1,0:T(8,128)S(1)}, f32[32,16,16,128]{3,2,1,0:T(8,128)}, u32[]{:S(2)}) %copy-start.1) | copy-done | bytes 4194328
  4.8 0.0 copy-start.2
  4.8 0.9 copy-done.2
  5.7 165.6 %exchange.1 = (bf16[2,44,3,128,128]{4,3,2,1,0:T(8,128)(2,1)}, f32[2,128,128]{2,1,0:T(8,128)S(1)}) custom-call(f32[32,16,16,128]{3,2,1,0:T(8,128)S(1)} %copy-done.1, f32[16,16,128]{2,1,0:T(8,128)S(1)} %copy-done.2, s32[4,8,128]{2,1,0:T(8,128)S(1)} %broadcast_in_dim.22.refs_2_), custom_call_target="tpu_custom_call" | custom-call | tf_op jit(solution)/shard_map/exchange/pallas_call | solution.py:224
  171.4 0.0 copy-start
  171.4 3.4 %copy-done = bf16[2,44,3,128,128]{4,3,2,1,0:T(8,128)(2,1)S(1)} copy-done((bf16[2,44,3,128,128]{4,3,2,1,0:T(8,128)(2,1)S(1)}, bf16[2,44,3,128,128]{4,3,2,1,0:T(8,128)(2,1)}, u32[]{:S(2)}) %copy-start) | copy-done | bytes 8650776
  174.8 18.4 %rows.1 = bf16[128,2,128,128]{3,2,1,0:T(8,128)(2,1)} custom-call(s32[512]{0:T(512)S(1)} %reshape.120.index, bf16[2,44,3,128,128]{4,3,2,1,0:T(8,128)(2,1)S(1)} %copy-done, f32[2,128,128]{2,1,0:T(8,128)S(1)} %get-tuple-element.8.weight), custom_call_target="tpu_custom_call" | custom-call | tf_op jit(solution)/shard_map/rows/pallas_call | solution.py:285
  (6 shorter events, 0.1 us)
Async XLA Ops:
  2.6 2.2 %copy-start.1 = (f32[32,16,16,128]{3,2,1,0:T(8,128)S(1)}, f32[32,16,16,128]{3,2,1,0:T(8,128)}, u32[]{:S(2)}) copy-start(f32[32,16,16,128]{3,2,1,0:T(8,128)} %refs_0_.1) | copy-start | bytes 12582916
  4.8 0.9 copy-start.2
  171.4 3.5 %copy-start = (bf16[2,44,3,128,128]{4,3,2,1,0:T(8,128)(2,1)S(1)}, bf16[2,44,3,128,128]{4,3,2,1,0:T(8,128)(2,1)}, u32[]{:S(2)}) copy-start(bf16[2,44,3,128,128]{4,3,2,1,0:T(8,128)(2,1)} %get-tuple-element.7.table) | copy-start | bytes 25952260

commit v2 on v1

--- a/solution.py
+++ b/solution.py
@@ -9,6 +9,7 @@
 
 MESH = pl.DeviceIdType.MESH
 REQ = 4
+PARTS = 4
 
 
 def lists(quadrupoles, per_group, groups):
@@ -19,7 +20,7 @@
     named = jnp.any(quadrupoles[:, 2:4].reshape(-1)[:, None] == ids[None, :], axis=0)
     before = (owner[:, None] == owner[None, :]) & (ids[None, :] < ids[:, None])
     rank = jnp.sum((before & named[None, :]).astype(jnp.int32), axis=1)
-    other = per_group + (away - 1) * REQ + jnp.minimum(rank, REQ - 1)
+    other = (away - 1) * REQ + jnp.minimum(rank, REQ - 1)
     slot = jnp.where(away == 0, ids - me * per_group, other)
     index = jnp.sum(jnp.where(quadrupoles[:, :, None] == ids, slot, 0), axis=-1)
     steps = jnp.arange(groups, dtype=jnp.int32)[:, None, None]
@@ -30,13 +31,17 @@
 
 
 def exchange_kernel(slabs, groups, planes, *refs):
-    pot, cond, asked, table_out, weight_out = refs[:5]
+    pot, cond, asked, index, out = refs[:5]
     pot_v, gz_src, asked_in, asked_s, weight_v = refs[5:10]
     p_in = refs[10 : 10 + planes]
     own = refs[10 + planes : 10 + 2 * planes]
-    far = refs[10 + 2 * planes : 10 + 3 * planes]
-    out_box = refs[10 + 3 * planes : 10 + 4 * planes]
-    (slab_send, slab_recv, cond_send, cond_recv, ask_send, ask_recv, far_send, far_recv, local) = refs[10 + 4 * planes :]
+    stop = 10 + 2 * planes + planes * PARTS
+    far = refs[10 + 2 * planes : stop]
+    out_box = refs[stop : stop + planes * PARTS]
+    result = refs[stop + planes * PARTS : stop + planes * PARTS + 2]
+    (slab_send, slab_recv, cond_send, cond_recv, ask_send, ask_recv, far_send, far_recv, local) = refs[
+        stop + planes * PARTS + 2 :
+    ]
 
     count, depth, rows, width = pot.shape
     me = lax.axis_index("slab")
@@ -111,6 +116,9 @@
         cond.at[pl.ds(me * planes, planes)], weight_v.at[:, my_rows, :], local.at[1 + 2 * planes]
     )
 
+    for step in range(1, slabs):
+        cond_copy(step).start()
+    cond_local.start()
     for plane in range(planes):
         for step in range(1, slabs):
             p_copy(plane, step).start()
@@ -129,40 +137,36 @@
         for step in range(1, slabs):
             gz_copy(plane, step).start()
         gz_local(plane).start()
-    for step in range(1, slabs):
-        cond_copy(step).start()
-    cond_local.start()
-
     for copy in asks:
         copy.wait()
     to_scalar = pltpu.make_async_copy(asked_in, asked_s, local.at[2 + 2 * planes])
     to_scalar.start()
     to_scalar.wait()
 
+    for step in range(1, slabs):
+        cond_copy(step).wait_recv()
+    cond_local.wait()
+
     x_size = p_in[0].shape[1]
+    part = x_size // PARTS
+    readings = out.shape[0]
     row = lax.broadcasted_iota(jnp.int32, (x_size, width), 0)
     lane = lax.broadcasted_iota(jnp.int32, (x_size, width), 1)
 
-    def far_copy(plane, step):
+    def far_copy(chunk, step):
         return pltpu.make_async_remote_copy(
-            src_ref=out_box[plane].at[step - 1],
-            dst_ref=far[plane].at[groups - 1 - step],
-            send_sem=far_send.at[plane, step],
-            recv_sem=far_recv.at[plane, step],
+            src_ref=out_box[chunk].at[step - 1],
+            dst_ref=far[chunk].at[pl.ds((groups - 1 - step) * REQ, REQ)],
+            send_sem=far_send.at[chunk, step],
+            recv_sem=far_recv.at[chunk, step],
             device_id={"elec": lax.rem(group + step, groups)},
             device_id_type=MESH,
         )
 
-    def own_out(plane):
+    def result_copy(chunk):
+        plane, place = divmod(chunk, PARTS)
         return pltpu.make_async_copy(
-            own[plane], table_out.at[plane, pl.ds(0, count)], local.at[3 + 2 * planes + plane]
-        )
-
-    def far_out(plane, place):
-        return pltpu.make_async_copy(
-            far[plane].at[place],
-            table_out.at[plane, pl.ds(count + place * REQ, REQ)],
-            local.at[3 + 3 * planes + plane * (groups - 1) + place],
+            result[chunk % 2], out.at[:, plane, pl.ds(place * part, part), :], local.at[3 + 2 * planes + chunk % 2]
         )
 
     for plane in range(planes):
@@ -182,53 +186,71 @@
             left = jnp.where(lane > 0, pltpu.roll(p, 1, 1), 0.0)
             own[plane][e, 2] = ((right - left) * 0.5).astype(jnp.bfloat16)
 
+        for place in range(PARTS):
+            chunk = plane * PARTS + place
+            cut = pl.ds(place * part, part)
+            for step in range(1, groups):
+                for which in range(REQ):
+                    chosen = asked_s[groups - step, 0, which]
+                    for way in range(3):
+                        out_box[chunk][step - 1, which, way] = own[plane][chosen, way, cut, :]
+                far_copy(chunk, step).start()
+
+        for place in range(PARTS):
+            chunk = plane * PARTS + place
+            cut = pl.ds(place * part, part)
+            for step in range(1, groups):
+                far_copy(chunk, step).wait_recv()
+            if chunk >= 2:
+                result_copy(chunk - 2).wait()
+            weight = -weight_v[plane, cut, :]
+
+            @pl.loop(0, readings // 4)
+            def _(block, plane=plane, chunk=chunk, cut=cut, weight=weight):
+                for k in range(4):
+                    m = block * 4 + k
+                    a, b, c, d = index[4 * m], index[4 * m + 1], index[4 * m + 2], index[4 * m + 3]
+                    total = None
+                    for way in range(3):
+                        first = own[plane][a, way, cut, :].astype(jnp.float32)
+                        second = own[plane][b, way, cut, :].astype(jnp.float32)
+                        third = far[chunk][c, way].astype(jnp.float32)
+                        fourth = far[chunk][d, way].astype(jnp.float32)
+                        term = (first - second) * (third - fourth)
+                        total = term if total is None else total + term
+                    result[chunk % 2][m] = (weight * total).astype(jnp.bfloat16)
+
+            result_copy(chunk).start()
+
+    chunks = planes * PARTS
+    for chunk in range(max(chunks - 2, 0), chunks):
+        result_copy(chunk).wait()
+    for chunk in range(chunks):
         for step in range(1, groups):
-            for place in range(REQ):
-                chosen = asked_s[groups - step, 0, place]
-                for d in range(3):
-                    out_box[plane][step - 1, place, d] = own[plane][chosen, d]
-            far_copy(plane, step).start()
-        own_out(plane).start()
-
-    for step in range(1, slabs):
-        cond_copy(step).wait_recv()
-    cond_local.wait()
-    weight_done = pltpu.make_async_copy(weight_v, weight_out, local.at[2 + 2 * planes])
-    weight_done.start()
+            far_copy(chunk, step).wait_send()
     for plane in range(planes):
-        for step in range(1, groups):
-            far_copy(plane, step).wait_recv()
-            far_out(plane, groups - 1 - step).start()
-    for plane in range(planes):
-        own_out(plane).wait()
-        for place in range(groups - 1):
-            far_out(plane, place).wait()
-        for step in range(1, groups):
-            far_copy(plane, step).wait_send()
         for step in range(1, slabs):
             p_copy(plane, step).wait_send()
             gz_copy(plane, step).wait_send()
     for step in range(1, slabs):
         cond_copy(step).wait_send()
-    weight_done.wait()
-
-
-def exchange(potentials, conductivity, asked, slabs, groups):
+
+
+def exchange(potentials, conductivity, asked, index, slabs, groups):
     count, depth, rows, width = potentials.shape
+    readings = index.shape[0]
     planes = depth // slabs
     x_size = rows * slabs
-    table_rows = count + (groups - 1) * REQ
+    part = x_size // PARTS
     hbm = pl.BlockSpec(memory_space=pl.ANY)
     dma = pltpu.SemaphoreType.DMA
     bf16, f32 = jnp.bfloat16, jnp.float32
+    chunks = planes * PARTS
     return pl.pallas_call(
         functools.partial(exchange_kernel, slabs, groups, planes),
-        out_shape=[
-            jax.ShapeDtypeStruct((planes, table_rows, 3, x_size, width), bf16),
-            jax.ShapeDtypeStruct((planes, x_size, width), f32),
-        ],
-        in_specs=[hbm, hbm, pl.BlockSpec(memory_space=pltpu.VMEM)],
-        out_specs=[hbm, hbm],
+        out_shape=jax.ShapeDtypeStruct((readings, planes, x_size, width), bf16),
+        in_specs=[hbm, hbm, pl.BlockSpec(memory_space=pltpu.VMEM), pl.BlockSpec(memory_space=pltpu.SMEM)],
+        out_specs=hbm,
         scratch_shapes=[
             pltpu.VMEM((count, depth, rows, width), f32),
             pltpu.VMEM((planes, slabs, count, rows, width), bf16),
@@ -238,8 +260,9 @@
         ]
         + [pltpu.VMEM((count, x_size, width), f32)] * planes
         + [pltpu.VMEM((count, 3, x_size, width), bf16)] * planes
-        + [pltpu.VMEM((groups - 1, REQ, 3, x_size, width), bf16)] * planes
-        + [pltpu.VMEM((groups - 1, REQ, 3, x_size, width), bf16)] * planes
+        + [pltpu.VMEM(((groups - 1) * REQ, 3, part, width), bf16)] * chunks
+        + [pltpu.VMEM((groups - 1, REQ, 3, part, width), bf16)] * chunks
+        + [pltpu.VMEM((readings, part, width), bf16)] * 2
         + [
             dma((2, planes, slabs)),
             dma((2, planes, slabs)),
@@ -247,56 +270,15 @@
             dma((slabs,)),
             dma((groups,)),
             dma((groups,)),
-            dma((planes, groups)),
-            dma((planes, groups)),
-            dma((3 + 3 * planes + planes * (groups - 1),)),
+            dma((chunks, groups)),
+            dma((chunks, groups)),
+            dma((5 + 2 * planes,)),
         ],
         compiler_params=pltpu.CompilerParams(
-            collective_id=0, has_side_effects=True, vmem_limit_bytes=48 * 1024 * 1024
+            collective_id=0, has_side_effects=True, vmem_limit_bytes=61 * 1024 * 1024
         ),
         name="exchange",
-    )(potentials, conductivity, asked)
-
-
-def rows_kernel(index, table, weight, out):
-    w = -weight[0]
-    readings = out.shape[0]
-
-    def reading(m):
-        a, b, c, d = index[4 * m], index[4 * m + 1], index[4 * m + 2], index[4 * m + 3]
-        total = None
-        for way in range(3):
-            source = table[0, a, way].astype(jnp.float32) - table[0, b, way].astype(jnp.float32)
-            probe = table[0, c, way].astype(jnp.float32) - table[0, d, way].astype(jnp.float32)
-            term = source * probe
-            total = term if total is None else total + term
-        out[m, 0] = (w * total).astype(jnp.bfloat16)
-
-    @pl.loop(0, readings // 4)
-    def _(block):
-        for k in range(4):
-            reading(block * 4 + k)
-
-
-def jacobian_rows(index, table, weight):
-    planes, table_rows, ways, x_size, width = table.shape
-    readings = index.shape[0]
-    part = 32
-    return pl.pallas_call(
-        rows_kernel,
-        out_shape=jax.ShapeDtypeStruct((readings, planes, x_size, width), jnp.bfloat16),
-        grid_spec=pltpu.PrefetchScalarGridSpec(
-            num_scalar_prefetch=1,
-            grid=(planes, x_size // part),
-            in_specs=[
-                pl.BlockSpec((1, table_rows, ways, part, width), lambda z, x, _: (z, 0, 0, x, 0)),
-                pl.BlockSpec((1, part, width), lambda z, x, _: (z, x, 0)),
-            ],
-            out_specs=pl.BlockSpec((readings, 1, part, width), lambda z, x, _: (0, z, x, 0)),
-        ),
-        compiler_params=pltpu.CompilerParams(vmem_limit_bytes=32 * 1024 * 1024),
-        name="rows",
-    )(index.reshape(-1), table, weight)
+    )(potentials, conductivity, asked, index.reshape(-1))
 
 
 def general(potentials, conductivity, quadrupoles):
@@ -331,11 +313,10 @@
 def shards(potentials, conductivity, quadrupoles):
     slabs, groups = lax.axis_size("slab"), lax.axis_size("elec")
     count, depth, rows, width = potentials.shape
-    if rows % 16 or width % 128 or depth % slabs or (rows * slabs) % 32 or quadrupoles.shape[0] % 4:
+    if rows % 16 or width % 128 or depth % slabs or (rows * slabs) % (16 * PARTS) or quadrupoles.shape[0] % 4:
         return general(potentials, conductivity, quadrupoles)
     index, asked = lists(quadrupoles, count, groups)
-    table, weight = exchange(potentials, conductivity, asked, slabs, groups)
-    return jacobian_rows(index, table, weight)
+    return exchange(potentials, conductivity, asked, index, slabs, groups)
 
 
 def solution(mesh):

time: 193 us -> 185 us (0.959)
  Pallas kernels: 184 us -> 170 us
  local copies, waits for them, and re-layouts: 7.7 us -> 12.9 us
    pallas_call x1 -> x0, Pallas kernels: 18.4 us -> none  [jacobian_rows(): pl.pallas_call(rows_kernel, out_shape=jax.ShapeDtypeStruct((readings, pla...]
    pallas_call x1, Pallas kernels: 166 us -> 170 us  [exchange(): pl.pallas_call(functools.partial(exchange_kernel, slabs, groups, planes),...]
    unnamed x6 -> x1, local copies, waits for them, and re-layouts: 6.54 us -> 10.5 us
where the time goes in v2:
time: 185 us; the launch traced here: 184 us
  Pallas kernels  170 us (92%)
  local copies, waits for them, and re-layouts  12.9 us (7%)
    pallas_call x1, Pallas kernels, exchange(): pl.pallas_call(functools.partial(exchange_kernel, slabs, groups, planes),...  170 us
    unnamed x1, local copies, waits for them, and re-layouts  10.5 us

profile of v2, /device:TPU:11, one launch (start us, length us, event | category | flops | bytes accessed | tf_op | source)
XLA Modules:
  0.0 184.4 jit_solution(816069671026172827)
XLA Ops:
  0.0 0.7 slice.3
  0.7 0.1 copy.7
  0.8 0.1 eq.84
  0.9 0.1 fusion
  1.1 0.2 convert_reduce_fusion
  1.3 0.9 select_reduce_fusion
  2.2 0.1 select_reduce_fusion.1
  2.4 0.6 broadcast_in_dim.18.refs_2_
  3.0 0.1 copy.8
  3.1 0.7 reshape.120.refs_3_
  3.8 170.1 %exchange.1 = bf16[128,2,128,128]{3,2,1,0:T(8,128)(2,1)} custom-call(f32[32,16,16,128]{3,2,1,0:T(8,128)} %refs_0_.1, f32[16,16,128]{2,1,0:T(8,128)} %refs_1_.1, s32[4,8,128]{2,1,0:T(8,128)} %broadcast_in_dim.18.refs_2_, s32[512]{0:T(512)} %reshape.120.refs_3_), custom_call_target="tpu_custom_call" | custom-call | tf_op jit(solution)/shard_map/exchange/pallas_call | solution.py:249
  173.9 10.5 %copy.10 = bf16[128,2,128,128]{3,2,1,0:T(8,128)(2,1)} copy(bf16[128,2,128,128]{3,2,1,0:T(8,128)(2,1)} %exchange.1) | data formatting | bytes 16777216
  (5 shorter events, 0.1 us)

commit v3 on v2

--- a/solution.py
+++ b/solution.py
@@ -30,18 +30,24 @@
     return index.astype(jnp.int32), jnp.broadcast_to(asked[:, None, :], (groups, 8, 128))
 
 
+def minus(first, second):
+    return first.astype(jnp.float32) - second.astype(jnp.float32)
+
+
 def exchange_kernel(slabs, groups, planes, *refs):
     pot, cond, asked, index, out = refs[:5]
     pot_v, gz_src, asked_in, asked_s, weight_v = refs[5:10]
     p_in = refs[10 : 10 + planes]
-    own = refs[10 + planes : 10 + 2 * planes]
-    stop = 10 + 2 * planes + planes * PARTS
-    far = refs[10 + 2 * planes : stop]
-    out_box = refs[stop : stop + planes * PARTS]
-    result = refs[stop + planes * PARTS : stop + planes * PARTS + 2]
-    (slab_send, slab_recv, cond_send, cond_recv, ask_send, ask_recv, far_send, far_recv, local) = refs[
-        stop + planes * PARTS + 2 :
-    ]
+    rest = list(refs[10 + planes :])
+
+    def take(n):
+        taken = rest[:n]
+        del rest[:n]
+        return taken
+
+    own_z, own_xy, far_xy, box_xy = take(planes), take(planes), take(planes), take(planes)
+    far_z, box_z, result = take(planes * PARTS), take(planes * PARTS), take(2)
+    slab_send, slab_recv, cond_send, cond_recv, ask_send, ask_recv, xy_send, xy_recv, far_send, far_recv, local = rest
 
     count, depth, rows, width = pot.shape
     me = lax.axis_index("slab")
@@ -86,7 +92,7 @@
         to = lax.rem(me + step, slabs)
         return pltpu.make_async_remote_copy(
             src_ref=gz_src.at[plane, to],
-            dst_ref=own[plane].at[:, 0, my_rows, :],
+            dst_ref=own_z[plane].at[:, my_rows, :],
             send_sem=slab_send.at[1, plane, step],
             recv_sem=slab_recv.at[1, plane, step],
             device_id={"slab": to},
@@ -109,7 +115,7 @@
 
     def gz_local(plane):
         return pltpu.make_async_copy(
-            gz_src.at[plane, me], own[plane].at[:, 0, my_rows, :], local.at[1 + planes + plane]
+            gz_src.at[plane, me], own_z[plane].at[:, my_rows, :], local.at[1 + planes + plane]
         )
 
     cond_local = pltpu.make_async_copy(
@@ -155,10 +161,20 @@
 
     def far_copy(chunk, step):
         return pltpu.make_async_remote_copy(
-            src_ref=out_box[chunk].at[step - 1],
-            dst_ref=far[chunk].at[pl.ds((groups - 1 - step) * REQ, REQ)],
+            src_ref=box_z[chunk].at[step - 1],
+            dst_ref=far_z[chunk].at[pl.ds((groups - 1 - step) * REQ, REQ)],
             send_sem=far_send.at[chunk, step],
             recv_sem=far_recv.at[chunk, step],
+            device_id={"elec": lax.rem(group + step, groups)},
+            device_id_type=MESH,
+        )
+
+    def xy_copy(plane, step):
+        return pltpu.make_async_remote_copy(
+            src_ref=box_xy[plane].at[step - 1],
+            dst_ref=far_xy[plane].at[pl.ds((groups - 1 - step) * REQ, REQ)],
+            send_sem=xy_send.at[plane, step],
+            recv_sem=xy_recv.at[plane, step],
             device_id={"elec": lax.rem(group + step, groups)},
             device_id_type=MESH,
         )
@@ -172,19 +188,28 @@
     for plane in range(planes):
         for step in range(1, slabs):
             p_copy(plane, step).wait_recv()
-            gz_copy(plane, step).wait_recv()
         p_local(plane).wait()
-        gz_local(plane).wait()
 
         @pl.loop(0, count)
         def _(e, plane=plane):
             p = p_in[plane][e]
             up = jnp.where(row < x_size - 1, pltpu.roll(p, x_size - 1, 0), 0.0)
             down = jnp.where(row > 0, pltpu.roll(p, 1, 0), 0.0)
-            own[plane][e, 1] = ((up - down) * 0.5).astype(jnp.bfloat16)
+            own_xy[plane][e, 0] = ((up - down) * 0.5).astype(jnp.bfloat16)
             right = jnp.where(lane < width - 1, pltpu.roll(p, width - 1, 1), 0.0)
             left = jnp.where(lane > 0, pltpu.roll(p, 1, 1), 0.0)
-            own[plane][e, 2] = ((right - left) * 0.5).astype(jnp.bfloat16)
+            own_xy[plane][e, 1] = ((right - left) * 0.5).astype(jnp.bfloat16)
+
+        for step in range(1, groups):
+            for which in range(REQ):
+                chosen = asked_s[groups - step, 0, which]
+                for way in range(2):
+                    box_xy[plane][step - 1, which, way] = own_xy[plane][chosen, way]
+            xy_copy(plane, step).start()
+
+        for step in range(1, slabs):
+            gz_copy(plane, step).wait_recv()
+        gz_local(plane).wait()
 
         for place in range(PARTS):
             chunk = plane * PARTS + place
@@ -192,10 +217,11 @@
             for step in range(1, groups):
                 for which in range(REQ):
                     chosen = asked_s[groups - step, 0, which]
-                    for way in range(3):
-                        out_box[chunk][step - 1, which, way] = own[plane][chosen, way, cut, :]
+                    box_z[chunk][step - 1, which] = own_z[plane][chosen, cut, :]
                 far_copy(chunk, step).start()
 
+        for step in range(1, groups):
+            xy_copy(plane, step).wait_recv()
         for place in range(PARTS):
             chunk = plane * PARTS + place
             cut = pl.ds(place * part, part)
@@ -210,14 +236,13 @@
                 for k in range(4):
                     m = block * 4 + k
                     a, b, c, d = index[4 * m], index[4 * m + 1], index[4 * m + 2], index[4 * m + 3]
-                    total = None
-                    for way in range(3):
-                        first = own[plane][a, way, cut, :].astype(jnp.float32)
-                        second = own[plane][b, way, cut, :].astype(jnp.float32)
-                        third = far[chunk][c, way].astype(jnp.float32)
-                        fourth = far[chunk][d, way].astype(jnp.float32)
-                        term = (first - second) * (third - fourth)
-                        total = term if total is None else total + term
+                    first, second = own_z[plane][a, cut, :], own_z[plane][b, cut, :]
+                    third, fourth = far_z[chunk][c], far_z[chunk][d]
+                    total = minus(first, second) * minus(third, fourth)
+                    for way in range(2):
+                        first, second = own_xy[plane][a, way, cut, :], own_xy[plane][b, way, cut, :]
+                        third, fourth = far_xy[plane][c, way, cut, :], far_xy[plane][d, way, cut, :]
+                        total = total + minus(first, second) * minus(third, fourth)
                     result[chunk % 2][m] = (weight * total).astype(jnp.bfloat16)
 
             result_copy(chunk).start()
@@ -229,6 +254,8 @@
         for step in range(1, groups):
             far_copy(chunk, step).wait_send()
     for plane in range(planes):
+        for step in range(1, groups):
+            xy_copy(plane, step).wait_send()
         for step in range(1, slabs):
             p_copy(plane, step).wait_send()
             gz_copy(plane, step).wait_send()
@@ -259,9 +286,12 @@
             pltpu.VMEM((planes, x_size, width), f32),
         ]
         + [pltpu.VMEM((count, x_size, width), f32)] * planes
-        + [pltpu.VMEM((count, 3, x_size, width), bf16)] * planes
-        + [pltpu.VMEM(((groups - 1) * REQ, 3, part, width), bf16)] * chunks
-        + [pltpu.VMEM((groups - 1, REQ, 3, part, width), bf16)] * chunks
+        + [pltpu.VMEM((count, x_size, width), bf16)] * planes
+        + [pltpu.VMEM((count, 2, x_size, width), bf16)] * planes
+        + [pltpu.VMEM(((groups - 1) * REQ, 2, x_size, width), bf16)] * planes
+        + [pltpu.VMEM((groups - 1, REQ, 2, x_size, width), bf16)] * planes
+        + [pltpu.VMEM(((groups - 1) * REQ, part, width), bf16)] * chunks
+        + [pltpu.VMEM((groups - 1, REQ, part, width), bf16)] * chunks
         + [pltpu.VMEM((readings, part, width), bf16)] * 2
         + [
             dma((2, planes, slabs)),
@@ -270,15 +300,41 @@
             dma((slabs,)),
             dma((groups,)),
             dma((groups,)),
+            dma((planes, groups)),
+            dma((planes, groups)),
             dma((chunks, groups)),
             dma((chunks, groups)),
             dma((5 + 2 * planes,)),
         ],
         compiler_params=pltpu.CompilerParams(
-            collective_id=0, has_side_effects=True, vmem_limit_bytes=61 * 1024 * 1024
+            collective_id=0, has_side_effects=True, vmem_limit_bytes=29 * 1024 * 1024
         ),
         name="exchange",
     )(potentials, conductivity, asked, index.reshape(-1))
+
+
+def deliver_kernel(source, target, done):
+    share = source.shape[0] // PARTS
+    copies = [
+        pltpu.make_async_copy(source.at[pl.ds(k * share, share)], target.at[pl.ds(k * share, share)], done.at[k])
+        for k in range(PARTS)
+    ]
+    for copy in copies:
+        copy.start()
+    for copy in copies:
+        copy.wait()
+
+
+def deliver(rows):
+    return pl.pallas_call(
+        deliver_kernel,
+        out_shape=jax.ShapeDtypeStruct(rows.shape, rows.dtype),
+        in_specs=[pl.BlockSpec(memory_space=pl.ANY)],
+        out_specs=pl.BlockSpec(memory_space=pl.ANY),
+        scratch_shapes=[pltpu.SemaphoreType.DMA((PARTS,))],
+        compiler_params=pltpu.CompilerParams(vmem_limit_bytes=1024 * 1024),
+        name="deliver",
+    )(rows)
 
 
 def general(potentials, conductivity, quadrupoles):
@@ -316,7 +372,7 @@
     if rows % 16 or width % 128 or depth % slabs or (rows * slabs) % (16 * PARTS) or quadrupoles.shape[0] % 4:
         return general(potentials, conductivity, quadrupoles)
     index, asked = lists(quadrupoles, count, groups)
-    return exchange(potentials, conductivity, asked, index, slabs, groups)
+    return deliver(exchange(potentials, conductivity, asked, index, slabs, groups))
 
 
 def solution(mesh):

time: 185 us -> 171 us (0.924)
  local copies, waits for them, and re-layouts: 12.9 us -> 4.25 us
  Pallas kernels: 170 us -> 165 us
    pallas_call x1, Pallas kernels: 170 us -> 162 us  [exchange(): pl.pallas_call(functools.partial(exchange_kernel, slabs, groups, planes),...]
    unnamed x1 -> x4, local copies, waits for them, and re-layouts: 10.5 us -> 3.09 us
    pallas_call x0 -> x1, Pallas kernels: none -> 3.37 us  [deliver(): pl.pallas_call(deliver_kernel, out_shape=jax.ShapeDtypeStruct(rows.shape,...]
where the time goes in v3:
time: 171 us
  Pallas kernels  165 us (96%)
  local copies, waits for them, and re-layouts  4.25 us (2%)
    pallas_call x1, Pallas kernels, exchange(): pl.pallas_call(functools.partial(exchange_kernel, slabs, groups, planes),...  162 us

profile of v3, /device:TPU:11, one launch (start us, length us, event | category | flops | bytes accessed | tf_op | source)
XLA Modules:
  0.0 170.9 jit_solution(6941391131657923434)
XLA Ops:
  0.0 0.7 slice.3
  0.7 0.1 copy.7
  0.8 0.1 eq.84
  0.9 0.1 fusion
  1.1 0.2 convert_reduce_fusion
  1.3 0.9 select_reduce_fusion
  2.2 0.1 select_reduce_fusion.1
  2.4 0.1 copy.8
  2.5 0.1 reshape.120.refs_3_
  2.6 0.0 copy-start
  2.6 2.2 %copy-done = f32[32,16,16,128]{3,2,1,0:T(8,128)S(1)} copy-done((f32[32,16,16,128]{3,2,1,0:T(8,128)S(1)}, f32[32,16,16,128]{3,2,1,0:T(8,128)}, u32[]{:S(2)}) %copy-start) | copy-done | bytes 4194328
  4.8 0.0 copy-start.1
  4.8 0.9 copy-done.1
  5.7 161.8 %exchange.1.source = bf16[128,2,128,128]{3,2,1,0:T(8,128)(2,1)S(1)} custom-call(f32[32,16,16,128]{3,2,1,0:T(8,128)S(1)} %copy-done, f32[16,16,128]{2,1,0:T(8,128)S(1)} %copy-done.1, s32[4,8,128]{2,1,0:T(8,128)S(1)} %broadcast_in_dim.18.refs_2_, s32[512]{0:T(512)S(1)} %reshape.120.refs_3_), custom_call_target="tpu_custom_call" | custom-call | tf_op jit(solution)/shard_map/exchange/pallas_call | solution.py:276
  167.5 3.4 %deliver.1 = bf16[128,2,128,128]{3,2,1,0:T(8,128)(2,1)} custom-call(bf16[128,2,128,128]{3,2,1,0:T(8,128)(2,1)S(1)} %exchange.1.source), custom_call_target="tpu_custom_call" | custom-call | tf_op jit(solution)/shard_map/deliver/pallas_call | solution.py:329
  (6 shorter events, 0.1 us)
Async XLA Ops:
  2.6 2.2 %copy-start = (f32[32,16,16,128]{3,2,1,0:T(8,128)S(1)}, f32[32,16,16,128]{3,2,1,0:T(8,128)}, u32[]{:S(2)}) copy-start(f32[32,16,16,128]{3,2,1,0:T(8,128)} %refs_0_.1) | copy-start | bytes 12582916
  4.8 0.9 copy-start.1

commit v4 on v3

--- a/solution.py
+++ b/solution.py
@@ -52,6 +52,7 @@
     count, depth, rows, width = pot.shape
     me = lax.axis_index("slab")
     group = lax.axis_index("elec")
+    far_first = sorted(range(1, slabs), key=lambda step: abs(2 * step - slabs))
     my_rows = pl.ds(pl.multiple_of(me * rows, rows), rows)
 
     stage = pltpu.make_async_copy(pot, pot_v, local.at[0])
@@ -126,7 +127,7 @@
         cond_copy(step).start()
     cond_local.start()
     for plane in range(planes):
-        for step in range(1, slabs):
+        for step in far_first:
             p_copy(plane, step).start()
         p_local(plane).start()
         if plane == 0:
@@ -140,7 +141,7 @@
                 below = pot_v[e, z - 1] if z > 0 else jnp.zeros((rows, width), jnp.float32)
                 gz_src[plane, to, e] = ((above - below) * 0.5).astype(jnp.bfloat16)
 
-        for step in range(1, slabs):
+        for step in far_first:
             gz_copy(plane, step).start()
         gz_local(plane).start()
     for copy in asks:

time: 171 us -> 172 us (level)
  no operation moved by 1% of the time
where the time goes in v4:
time: 172 us
  Pallas kernels  166 us (97%)
  local copies, waits for them, and re-layouts  4.25 us (2%)
    pallas_call x1, Pallas kernels, exchange(): pl.pallas_call(functools.partial(exchange_kernel, slabs, groups, planes),...  163 us

profile of v4, /device:TPU:11, one launch (start us, length us, event | category | flops | bytes accessed | tf_op | source)
XLA Modules:
  0.0 171.8 jit_solution(3118660361629068169)
XLA Ops:
  0.0 0.7 slice.3
  0.7 0.1 copy.7
  0.8 0.1 eq.84
  0.9 0.1 fusion
  1.1 0.2 convert_reduce_fusion
  1.3 0.9 select_reduce_fusion
  2.2 0.1 select_reduce_fusion.1
  2.4 0.1 copy.8
  2.5 0.1 reshape.120.refs_3_
  2.6 0.0 copy-start
  2.6 2.2 %copy-done = f32[32,16,16,128]{3,2,1,0:T(8,128)S(1)} copy-done((f32[32,16,16,128]{3,2,1,0:T(8,128)S(1)}, f32[32,16,16,128]{3,2,1,0:T(8,128)}, u32[]{:S(2)}) %copy-start) | copy-done | bytes 4194328
  4.8 0.0 copy-start.1
  4.8 0.9 copy-done.1
  5.7 162.7 %exchange.1.source = bf16[128,2,128,128]{3,2,1,0:T(8,128)(2,1)S(1)} custom-call(f32[32,16,16,128]{3,2,1,0:T(8,128)S(1)} %copy-done, f32[16,16,128]{2,1,0:T(8,128)S(1)} %copy-done.1, s32[4,8,128]{2,1,0:T(8,128)S(1)} %broadcast_in_dim.18.refs_2_, s32[512]{0:T(512)S(1)} %reshape.120.refs_3_), custom_call_target="tpu_custom_call" | custom-call | tf_op jit(solution)/shard_map/exchange/pallas_call | solution.py:277
  168.4 3.4 %deliver.1 = bf16[128,2,128,128]{3,2,1,0:T(8,128)(2,1)} custom-call(bf16[128,2,128,128]{3,2,1,0:T(8,128)(2,1)S(1)} %exchange.1.source), custom_call_target="tpu_custom_call" | custom-call | tf_op jit(solution)/shard_map/deliver/pallas_call | solution.py:330
  (6 shorter events, 0.1 us)
Async XLA Ops:
  2.6 2.2 %copy-start = (f32[32,16,16,128]{3,2,1,0:T(8,128)S(1)}, f32[32,16,16,128]{3,2,1,0:T(8,128)}, u32[]{:S(2)}) copy-start(f32[32,16,16,128]{3,2,1,0:T(8,128)} %refs_0_.1) | copy-start | bytes 12582916
  4.8 0.9 copy-start.1

commit v5 on v3

--- a/solution.py
+++ b/solution.py
@@ -36,9 +36,9 @@
 
 def exchange_kernel(slabs, groups, planes, *refs):
     pot, cond, asked, index, out = refs[:5]
-    pot_v, gz_src, asked_in, asked_s, weight_v = refs[5:10]
-    p_in = refs[10 : 10 + planes]
-    rest = list(refs[10 + planes :])
+    gz_src, asked_in, asked_s, weight_v = refs[5:9]
+    p_in = refs[9 : 9 + planes]
+    rest = list(refs[9 + planes :])
 
     def take(n):
         taken = rest[:n]
@@ -53,9 +53,6 @@
     me = lax.axis_index("slab")
     group = lax.axis_index("elec")
     my_rows = pl.ds(pl.multiple_of(me * rows, rows), rows)
-
-    stage = pltpu.make_async_copy(pot, pot_v, local.at[0])
-    stage.start()
 
     barrier = pltpu.get_barrier_semaphore()
     for step in range(1, slabs):
@@ -129,15 +126,13 @@
         for step in range(1, slabs):
             p_copy(plane, step).start()
         p_local(plane).start()
-        if plane == 0:
-            stage.wait()
 
         @pl.loop(0, count)
         def _(e, plane=plane):
             for to in range(slabs):
                 z = to * planes + plane
-                above = pot_v[e, z + 1] if z + 1 < depth else jnp.zeros((rows, width), jnp.float32)
-                below = pot_v[e, z - 1] if z > 0 else jnp.zeros((rows, width), jnp.float32)
+                above = pot[e, z + 1] if z + 1 < depth else jnp.zeros((rows, width), jnp.float32)
+                below = pot[e, z - 1] if z > 0 else jnp.zeros((rows, width), jnp.float32)
                 gz_src[plane, to, e] = ((above - below) * 0.5).astype(jnp.bfloat16)
 
         for step in range(1, slabs):
@@ -276,10 +271,9 @@
     return pl.pallas_call(
         functools.partial(exchange_kernel, slabs, groups, planes),
         out_shape=jax.ShapeDtypeStruct((readings, planes, x_size, width), bf16),
-        in_specs=[hbm, hbm, pl.BlockSpec(memory_space=pltpu.VMEM), pl.BlockSpec(memory_space=pltpu.SMEM)],
+        in_specs=[pl.BlockSpec(memory_space=pltpu.VMEM), hbm, pl.BlockSpec(memory_space=pltpu.VMEM), pl.BlockSpec(memory_space=pltpu.SMEM)],
         out_specs=hbm,
         scratch_shapes=[
-            pltpu.VMEM((count, depth, rows, width), f32),
             pltpu.VMEM((planes, slabs, count, rows, width), bf16),
             pltpu.VMEM((groups, 8, 128), jnp.int32),
             pltpu.SMEM((groups, 8, 128), jnp.int32),

time: 171 us -> 171 us (level)
  no operation moved by 1% of the time
where the time goes in v5:
time: 171 us
  Pallas kernels  165 us (96%)
  local copies, waits for them, and re-layouts  4.25 us (2%)
    pallas_call x1, Pallas kernels, exchange(): pl.pallas_call(functools.partial(exchange_kernel, slabs, groups, planes),...  162 us

profile of v5, /device:TPU:11, one launch (start us, length us, event | category | flops | bytes accessed | tf_op | source)
XLA Modules:
  0.0 170.6 jit_solution(8236972215244534437)
XLA Ops:
  0.0 0.7 slice.3
  0.7 0.1 copy.7
  0.8 0.1 eq.84
  0.9 0.1 fusion
  1.1 0.2 convert_reduce_fusion
  1.3 0.9 select_reduce_fusion
  2.2 0.1 select_reduce_fusion.1
  2.4 0.1 copy.8
  2.5 0.1 reshape.120.refs_3_
  2.6 0.0 copy-start
  2.6 2.2 %copy-done = f32[32,16,16,128]{3,2,1,0:T(8,128)S(1)} copy-done((f32[32,16,16,128]{3,2,1,0:T(8,128)S(1)}, f32[32,16,16,128]{3,2,1,0:T(8,128)}, u32[]{:S(2)}) %copy-start) | copy-done | bytes 4194328
  4.8 0.0 copy-start.1
  4.8 0.9 copy-done.1
  5.7 161.5 %exchange.1.source = bf16[128,2,128,128]{3,2,1,0:T(8,128)(2,1)S(1)} custom-call(f32[32,16,16,128]{3,2,1,0:T(8,128)S(1)} %copy-done, f32[16,16,128]{2,1,0:T(8,128)S(1)} %copy-done.1, s32[4,8,128]{2,1,0:T(8,128)S(1)} %broadcast_in_dim.18.refs_2_, s32[512]{0:T(512)S(1)} %reshape.120.refs_3_), custom_call_target="tpu_custom_call" | custom-call | tf_op jit(solution)/shard_map/exchange/pallas_call | solution.py:271
  167.2 3.4 %deliver.1 = bf16[128,2,128,128]{3,2,1,0:T(8,128)(2,1)} custom-call(bf16[128,2,128,128]{3,2,1,0:T(8,128)(2,1)S(1)} %exchange.1.source), custom_call_target="tpu_custom_call" | custom-call | tf_op jit(solution)/shard_map/deliver/pallas_call | solution.py:323
  (6 shorter events, 0.1 us)
Async XLA Ops:
  2.6 2.2 %copy-start = (f32[32,16,16,128]{3,2,1,0:T(8,128)S(1)}, f32[32,16,16,128]{3,2,1,0:T(8,128)}, u32[]{:S(2)}) copy-start(f32[32,16,16,128]{3,2,1,0:T(8,128)} %refs_0_.1) | copy-start | bytes 12582916
  4.8 0.9 copy-start.1
